TPU v7x, 32 devices: a whole 2x2x4 slice. The times are simulated.
32 devices in a mesh: ctx: 8 (over z, x), head: 4 (over y, core).
Axes of the slice: x: 2, y: 2, z: 4, core: 2. Of those that a mesh axis runs over, the one named last changes fastest.
Arguments:
- queries: bfloat16 [16, 256, 5120], P('head', 'ctx'), may hold values from -32 to 32
- keys: bfloat16 [16, 256, 5120], P('head', 'ctx'), may hold values from -32 to 32
- values: bfloat16 [16, 256, 5120], P('head', 'ctx'), may hold values from -6 to 6
- out_grad: bfloat16 [16, 256, 5120], P('head', 'ctx'), may hold values from -6 to 6
- band_frames: int32 [16, 8, 8], P(None, 'ctx'), may hold values from -1 to 15, as said below
- frame_order: int32 [16], replicated, may hold values from 0 to 15, each once
Outputs:
- attended: bfloat16 [16, 256, 5120], P('head', 'ctx')
- query_grad: bfloat16 [16, 256, 5120], P('head', 'ctx')
- key_grad: bfloat16 [16, 256, 5120], P('head', 'ctx')
- value_grad: bfloat16 [16, 256, 5120], P('head', 'ctx')
Inputs may be any that keep to these rules, and one draw needn't show every extreme that they name: `band_frames`: entry [f, c, 2 b + r] is f - d for r = 0 or f + d for r = 1, with 2**b <= d < 2**(b+1), or -1 where that frame lies outside 0 to 15. `frame_order`: each frame once.
All inputs are finite; a program needn't handle non-finite values.
Results may differ from a plain program's by a relative error of at most 0.012.
Values may be sent and summed in bfloat16 or wider, within the bound.
A program may use at most 192 MiB of HBM per device.

v0:
```python
import jax
import jax.numpy as jnp
from jax import lax
from jax.sharding import PartitionSpec as P

HEADS = 40
HD = 128


NEGATIVE = -1e30
GROUP = 4


def extended_2(value, sides, width):
    for axis, dim in sides:
        count, length = (lax.axis_size(axis), value.shape[dim])
        up = [(i, (i + 1) % count) for i in range(count - 1)]
        down = [(j, i) for i, j in up]
        last = lax.slice_in_dim(value, length - width, length, axis=dim)
        leading = lax.slice_in_dim(value, 0, width, axis=dim)
        before = lax.ppermute(last, axis, up)
        after = lax.ppermute(leading, axis, down)
        value = jnp.concatenate([before, value, after], axis=dim)
    return value


def passed_along(block, axis, distance):
    devices = range(lax.axis_size(axis))
    route = [(i - distance, i) for i in devices if i - distance in devices]
    return lax.ppermute(block, axis, route)


def far_positions(slot_frames, frame_order):
    count = frame_order.shape[0]
    frame_ids = jnp.arange(count, dtype=jnp.int32)
    one_hot = (frame_order[:, None] == frame_ids[None, :]).astype(jnp.int32)
    inverse = jnp.sum(one_hot * frame_ids[:, None], axis=0)
    picked = jnp.sum(one_hot[:, :, None] * slot_frames[None, :, :], axis=1)
    far_rows = jnp.sum(
        (picked[:, :, None] == frame_ids[None, None, :]).astype(jnp.int32) * inverse[None, None, :],
        axis=2,
    )
    return (far_rows, picked >= 0)


def masked_scores(query_block, key_block, key_mask, score_scale):
    scores = (
        jnp.einsum("gqhd,gkhd->ghqk", query_block, key_block, preferred_element_type=jnp.float32)
        * score_scale
    )
    return jnp.where(key_mask[:, None, None, :], scores, NEGATIVE)


def forward_group(query_block, key_block, value_block, key_mask, score_scale):
    scores = masked_scores(query_block, key_block, key_mask, score_scale)
    highest = jnp.max(scores, axis=-1, keepdims=True)
    log_total = highest + jnp.log(jnp.sum(jnp.exp(scores - highest), axis=-1, keepdims=True))
    weights = jnp.exp(scores - log_total).astype(jnp.bfloat16)
    attended = jnp.einsum(
        "ghqk,gkhd->gqhd", weights, value_block, preferred_element_type=jnp.float32
    )
    return (attended.astype(jnp.bfloat16), log_total)


def backward_group(
    query_block,
    key_block,
    value_block,
    key_mask,
    grad_block,
    attended_block,
    log_block,
    score_scale,
):
    scores = masked_scores(query_block, key_block, key_mask, score_scale)
    softmax = jnp.exp(scores - log_block)
    weights = softmax.astype(jnp.bfloat16)
    row_delta = jnp.sum(
        grad_block.astype(jnp.float32) * attended_block.astype(jnp.float32), axis=-1
    )
    prob_grads = jnp.einsum(
        "gqhd,gkhd->ghqk", grad_block, value_block, preferred_element_type=jnp.float32
    )
    score_grads = (
        softmax * (prob_grads - jnp.transpose(row_delta, (0, 2, 1))[..., None]) * score_scale
    ).astype(jnp.bfloat16)
    query_grad = jnp.einsum(
        "ghqk,gkhd->gqhd", score_grads, key_block, preferred_element_type=jnp.float32
    ).astype(jnp.bfloat16)
    key_grad = jnp.einsum(
        "ghqk,gqhd->gkhd", score_grads, query_block, preferred_element_type=jnp.float32
    )
    value_grad = jnp.einsum(
        "ghqk,gqhd->gkhd", weights, grad_block, preferred_element_type=jnp.float32
    )
    return (query_grad, key_grad, value_grad)


def on_device(queries, keys, values, out_grad, band_frames, frame_order):
    head_count = HEADS // lax.axis_size("head")
    query_all, key_all, value_all, grad_all = (
        lax.all_to_all(queries, "head", split_axis=2, concat_axis=0, tiled=True),
        lax.all_to_all(keys, "head", split_axis=2, concat_axis=0, tiled=True),
        lax.all_to_all(values, "head", split_axis=2, concat_axis=0, tiled=True),
        lax.all_to_all(out_grad, "head", split_axis=2, concat_axis=0, tiled=True),
    )
    frame_count, slab_rows, columns = query_all.shape
    span_rows = slab_rows + 2 * slab_rows
    score_scale = HD ** (-0.5)
    group_count = frame_count // GROUP
    position = (
        lax.axis_index("ctx") * slab_rows - slab_rows + jnp.arange(span_rows, dtype=jnp.int32)
    )
    window_valid = (position >= 0) & (position < slab_rows * lax.axis_size("ctx"))
    far_rows, far_valid = far_positions(band_frames[:, 0, :], frame_order)
    band_count = far_rows.shape[1]
    key_count = span_rows + band_count * slab_rows
    four_dims = (GROUP, -1, head_count, HD)
    stacked = jnp.stack((key_all, value_all))
    extended = extended_2(stacked, (("ctx", 2),), slab_rows)

    def blocks(offset):
        rows_here = lax.dynamic_slice_in_dim(far_rows, offset, GROUP, 0)
        valid_here = lax.dynamic_slice_in_dim(far_valid, offset, GROUP, 0)
        window = lax.dynamic_slice_in_dim(extended, offset, GROUP, 1)
        far_keys = key_all[rows_here].reshape(GROUP, band_count * slab_rows, columns)
        far_values = value_all[rows_here].reshape(GROUP, band_count * slab_rows, columns)
        key_block = jnp.concatenate((window[0], far_keys), axis=1).reshape(four_dims)
        value_block = jnp.concatenate((window[1], far_values), axis=1).reshape(four_dims)
        key_mask = jnp.concatenate(
            (
                jnp.broadcast_to(window_valid[None, :], (GROUP, span_rows)),
                jnp.repeat(valid_here, slab_rows, axis=1),
            ),
            axis=1,
        )
        return (key_block, value_block, key_mask, rows_here)

    def forward_step(group_index):
        offset = group_index * GROUP
        query_block = lax.dynamic_slice_in_dim(query_all, offset, GROUP, 0).reshape(four_dims)
        key_block, value_block, key_mask, rows_here = blocks(offset)
        return forward_group(query_block, key_block, value_block, key_mask, score_scale)

    attended, log_total = lax.map(forward_step, jnp.arange(group_count, dtype=jnp.int32))
    attended = attended.reshape(frame_count, slab_rows, columns)
    log_total = log_total.reshape(frame_count, head_count, slab_rows, 1)

    def backward_step(carry, group_index):
        window_sum, far_sum = carry
        offset = group_index * GROUP
        query_block = lax.dynamic_slice_in_dim(query_all, offset, GROUP, 0).reshape(four_dims)
        grad_block = lax.dynamic_slice_in_dim(grad_all, offset, GROUP, 0).reshape(four_dims)
        attended_block = lax.dynamic_slice_in_dim(attended, offset, GROUP, 0).reshape(four_dims)
        log_block = lax.dynamic_slice_in_dim(log_total, offset, GROUP, 0)
        key_block, value_block, key_mask, rows_here = blocks(offset)
        query_grad, key_grad, value_grad = backward_group(
            query_block,
            key_block,
            value_block,
            key_mask,
            grad_block,
            attended_block,
            log_block,
            score_scale,
        )
        key_terms = jnp.stack((key_grad, value_grad)).reshape(2, GROUP, key_count, columns)
        window_sum = lax.dynamic_update_slice_in_dim(
            window_sum, key_terms[:, :, :span_rows], offset, 1
        )
        far_terms = key_terms[:, :, span_rows:].reshape(2, GROUP * band_count, slab_rows, columns)
        far_sum = far_sum.at[:, rows_here.reshape(-1)].add(far_terms)
        return ((window_sum, far_sum), query_grad.reshape(GROUP, slab_rows, columns))

    start = (
        jnp.zeros((2, frame_count, span_rows, columns), jnp.float32),
        jnp.zeros((2, frame_count, slab_rows, columns), jnp.float32),
    )
    (window_sum, far_sum), query_grad = lax.scan(
        backward_step, start, jnp.arange(group_count, dtype=jnp.int32)
    )
    query_grad = query_grad.reshape(frame_count, slab_rows, columns)
    center = window_sum[:, :, slab_rows : slab_rows + slab_rows] + far_sum
    lower_rim = window_sum[:, :, :slab_rows].astype(jnp.bfloat16)
    upper_rim = window_sum[:, :, slab_rows + slab_rows :].astype(jnp.bfloat16)
    from_above = passed_along(lower_rim, "ctx", -1)
    from_below = passed_along(upper_rim, "ctx", 1)
    center = center.at[:, :, slab_rows - slab_rows :].add(from_above.astype(jnp.float32))
    center = center.at[:, :, :slab_rows].add(from_below.astype(jnp.float32))
    key_grad = center[0].astype(jnp.bfloat16)
    value_grad = center[1].astype(jnp.bfloat16)
    leaving = (
        lax.all_to_all(attended, "head", split_axis=0, concat_axis=2, tiled=True),
        lax.all_to_all(query_grad, "head", split_axis=0, concat_axis=2, tiled=True),
        lax.all_to_all(key_grad, "head", split_axis=0, concat_axis=2, tiled=True),
        lax.all_to_all(value_grad, "head", split_axis=0, concat_axis=2, tiled=True),
    )
    return (leaving[0], leaving[1], leaving[2], leaving[3])


def solution(mesh):
    placed = (
        P("head", "ctx", None),
        P("head", "ctx", None),
        P("head", "ctx", None),
        P("head", "ctx", None),
        P(None, "ctx", None),
        P(),
    )
    return jax.shard_map(
        on_device,
        mesh=mesh,
        in_specs=placed,
        out_specs=(
            P("head", "ctx", None),
            P("head", "ctx", None),
            P("head", "ctx", None),
            P("head", "ctx", None),
        ),
        check_vma=False,
    )
```

profile of v0, /device:TPU:0, one launch (start us, length us, event | category | flops | bytes accessed | tf_op | source)
XLA Modules:
  0.0 1159.3 jit_solution(9441741861551341560)
XLA Ops:
  147.7 39.1 %collective-permute-done = bf16[2,16,32,1280]{3,2,1,0:T(8,128)(2,1)} collective-permute-done((bf16[2,16,32,1280]{3,2,1,0:T(8,128)(2,1)}, bf16[2,16,32,1280]{3,2,1,0:T(8,128)(2,1)}, u32[]{:S(2)}, u32[]{:S(2)}) %collective-permute-start) | collective-permute-done | bytes 2621472 | tf_op jit(solution)/shard_map/ppermute | solution.py:21
  192.8 13.9 %copy.147 = bf16[2,16,96,1280]{2,3,1,0:T(8,128)(2,1)} copy(bf16[2,16,96,1280]{3,2,1,0:T(8,128)(2,1)} %pad_maximum_fusion.11) | data formatting | bytes 15728640
  206.7 159.5 %while.32 = (s32[]{:T(128)}, bf16[4,4,32,10,128]{4,2,3,1,0:T(8,128)(2,1)}, f32[4,4,10,32,1]{3,2,1,4,0:T(8,128)}, s32[4]{0:T(128)S(1)}, bf16[2,16,96,1280]{2,3,1,...) while((s32[]{:T(128)}, ...), condition=%wide.region_6.7_spmd.clone, body=%wide.region_3.6_spmd.clone.sunk | while | flops 248424032 | bytes 74956752 | solution.py:145
  383.5 590.2 %while.33 = (s32[]{:T(128)}, f32[2,16,96,1280]{3,2,1,0:T(8,128)}, f32[2,16,32,1280]{3,2,1,0:T(8,128)}, bf16[4,4,32,1280]{3,2,1,0:T(8,128)(2,1)}, s32[4]{0:T(128)...) while((s32[]{:T(128)}, f32[2,16,96,1280]{3,2,1,0:T(8,128)}, ...), condition=%wide.region_10.11_spmd.clone, body=%wide.region_7.10_spmd.clone.sunk | while | flops 608995008 | bytes 271391296 | solution.py:179
  467.8 12.1 %pad_maximum_fusion.20 = f32[2,4,256,1280]{2,3,1,0:T(8,128)} fusion(f32[1,4,352,1280]{2,3,1,0:T(8,128)} %bitcast.174, f32[1,4,352,1280]{2,3,1,0:T(8,128)} %bitcast.176), kind=kLoop, calls=%fused_computation.36.clone.1 | loop fusion | flops 2621440 | bytes 24903680 | tf_op jit(solution)/shard_map/while/body/eval_jaxpr/stack | solution.py:167
  485.5 11.3 copy.228
  496.8 9.1 copy.229
  505.9 21.0 %scatter_fusion = f32[2,16,32,1280]{3,2,1,0:T(8,128)} fusion(f32[2,16,32,1280]{3,2,1,0:T(8,128)} %get-tuple-element.620, s32[32]{0:T(128)S(1)} %copy-done.13, f32[32,2,32,1280]{3,2,1,0:T(8,128)} %copy.229), kind=kCustom, calls=%fused_computation.4.clone.clone.1 | custom fusion | flops 2621440 | bytes 31457408 | tf_op jit(solution)/shard_map/while/body/eval_jaxpr/scatter-add | solution.py:172
  615.3 12.1 %pad_maximum_fusion.20 = f32[2,4,256,1280]{2,3,1,0:T(8,128)} fusion(f32[1,4,352,1280]{2,3,1,0:T(8,128)} %bitcast.174, f32[1,4,352,1280]{2,3,1,0:T(8,128)} %bitcast.176), kind=kLoop, calls=%fused_computation.36.clone.1 | loop fusion | flops 2621440 | bytes 24903680 | tf_op jit(solution)/shard_map/while/body/eval_jaxpr/stack | solution.py:167
  633.0 11.3 copy.228
  644.3 9.1 copy.229
  653.4 20.9 %scatter_fusion = f32[2,16,32,1280]{3,2,1,0:T(8,128)} fusion(f32[2,16,32,1280]{3,2,1,0:T(8,128)} %get-tuple-element.620, s32[32]{0:T(128)S(1)} %copy-done.13, f32[32,2,32,1280]{3,2,1,0:T(8,128)} %copy.229), kind=kCustom, calls=%fused_computation.4.clone.clone.1 | custom fusion | flops 2621440 | bytes 31457408 | tf_op jit(solution)/shard_map/while/body/eval_jaxpr/scatter-add | solution.py:172
  762.6 12.1 %pad_maximum_fusion.20 = f32[2,4,256,1280]{2,3,1,0:T(8,128)} fusion(f32[1,4,352,1280]{2,3,1,0:T(8,128)} %bitcast.174, f32[1,4,352,1280]{2,3,1,0:T(8,128)} %bitcast.176), kind=kLoop, calls=%fused_computation.36.clone.1 | loop fusion | flops 2621440 | bytes 24903680 | tf_op jit(solution)/shard_map/while/body/eval_jaxpr/stack | solution.py:167
  780.3 11.3 copy.228
  800.8 21.0 %scatter_fusion = f32[2,16,32,1280]{3,2,1,0:T(8,128)} fusion(f32[2,16,32,1280]{3,2,1,0:T(8,128)} %get-tuple-element.620, s32[32]{0:T(128)S(1)} %copy-done.13, f32[32,2,32,1280]{3,2,1,0:T(8,128)} %copy.229), kind=kCustom, calls=%fused_computation.4.clone.clone.1 | custom fusion | flops 2621440 | bytes 31457408 | tf_op jit(solution)/shard_map/while/body/eval_jaxpr/scatter-add | solution.py:172
  910.1 12.1 %pad_maximum_fusion.20 = f32[2,4,256,1280]{2,3,1,0:T(8,128)} fusion(f32[1,4,352,1280]{2,3,1,0:T(8,128)} %bitcast.174, f32[1,4,352,1280]{2,3,1,0:T(8,128)} %bitcast.176), kind=kLoop, calls=%fused_computation.36.clone.1 | loop fusion | flops 2621440 | bytes 24903680 | tf_op jit(solution)/shard_map/while/body/eval_jaxpr/stack | solution.py:167
  927.8 11.3 copy.228
  948.3 20.9 %scatter_fusion = f32[2,16,32,1280]{3,2,1,0:T(8,128)} fusion(f32[2,16,32,1280]{3,2,1,0:T(8,128)} %get-tuple-element.620, s32[32]{0:T(128)S(1)} %copy-done.13, f32[32,2,32,1280]{3,2,1,0:T(8,128)} %copy.229), kind=kCustom, calls=%fused_computation.4.clone.clone.1 | custom fusion | flops 2621440 | bytes 31457408 | tf_op jit(solution)/shard_map/while/body/eval_jaxpr/scatter-add | solution.py:172
  973.7 9.7 convert.9
  996.2 19.7 %all_to_all.144 = bf16[16,32,1280]{2,1,0:T(8,128)(2,1)S(1)} all-to-all(bf16[16,32,1280]{2,1,0:T(8,128)(2,1)S(1)} %copy-done.9), channel_id=1, replica_groups=mesh['ctx'=8,'head'=4] {'head'}, dimensions={0} | all-to-all | bytes 2621440 | tf_op jit(solution)/shard_map/all_to_all | solution.py:193
  1020.2 29.9 %collective-permute-done.2 = bf16[2,16,32,1280]{3,2,1,0:T(8,128)(2,1)} collective-permute-done((bf16[2,16,32,1280]{3,2,1,0:T(8,128)(2,1)}, bf16[2,16,32,1280]{3,2,1,0:T(8,128)(2,1)}, u32[]{:S(2)}, u32[]{:S(2)}) %collective-permute-start.2) | collective-permute-done | bytes 2621472 | tf_op jit(solution)/shard_map/ppermute | solution.py:30
  1050.1 56.3 %collective-permute-done.3 = bf16[2,16,32,1280]{3,2,1,0:T(8,128)(2,1)} collective-permute-done((bf16[2,16,32,1280]{3,2,1,0:T(8,128)(2,1)}, bf16[2,16,32,1280]{3,2,1,0:T(8,128)(2,1)}, u32[]{:S(2)}, u32[]{:S(2)}) %collective-permute-start.3) | collective-permute-done | bytes 2621472 | tf_op jit(solution)/shard_map/ppermute | solution.py:30
  1114.8 20.4 %all_to_all.145 = bf16[16,32,1280]{2,1,0:T(8,128)(2,1)} all-to-all(bf16[16,32,1280]{2,1,0:T(8,128)(2,1)S(1)} %get-tuple-element.362), channel_id=1, replica_groups=mesh['ctx'=8,'head'=4] {'head'}, dimensions={0} | all-to-all | bytes 2621440 | tf_op jit(solution)/shard_map/all_to_all | solution.py:196
  1145.4 10.7 all-to-all-done.6
  (441 shorter events, 755.5 us)
Async XLA Ops:
  15.2 4.4 copy-start.11
  15.2 21.6 %all-to-all-start = ((bf16[4,2,81920]{2,1,0:T(2,128)(2,1)}), bf16[4,2,81920]{2,1,0:T(2,128)(2,1)S(1)}, u32[]{:S(2)}, u32[]{:S(2)}) async-start(bf16[4,2,81920]{2,1,0:T(2,128)(2,1)} %reshape.318), calls=%async_computation | async-start | bytes 2621440 | tf_op jit(solution)/shard_map/all_to_all | solution.py:103
  36.8 20.8 %all-to-all-start.1 = ((bf16[4,2,81920]{2,1,0:T(2,128)(2,1)}), bf16[4,2,81920]{2,1,0:T(2,128)(2,1)S(1)}, u32[]{:S(2)}, u32[]{:S(2)}) async-start(bf16[4,2,81920]{2,1,0:T(2,128)(2,1)} %reshape.316), calls=%async_computation.1 | async-start | bytes 2621440 | tf_op jit(solution)/shard_map/all_to_all | solution.py:104
  69.4 78.3 %collective-permute-start.1 = (bf16[2,16,32,1280]{3,2,1,0:T(8,128)(2,1)}, bf16[2,16,32,1280]{3,2,1,0:T(8,128)(2,1)}, u32[]{:S(2)}, u32[]{:S(2)}) collective-permute-start(bf16[2,16,32,1280]{3,2,1,0:T(8,128)(2,1)} %pad_maximum_fusion.12), channel_id=1, source_target_pairs={{4,0},{8,4},{12,8},{16,12},{20,16},{24,20},{28,24},{5,1},{9,5},{13... | collective-permute-start | bytes 7864328 | tf_op jit(solution)/shard_map/ppermute | solution.py:22
  70.7 116.1 %collective-permute-start = (bf16[2,16,32,1280]{3,2,1,0:T(8,128)(2,1)}, bf16[2,16,32,1280]{3,2,1,0:T(8,128)(2,1)}, u32[]{:S(2)}, u32[]{:S(2)}) collective-permute-start(bf16[2,16,32,1280]{3,2,1,0:T(8,128)(2,1)} %pad_maximum_fusion.12), channel_id=1, source_target_pairs={{0,4},{4,8},{8,12},{12,16},{16,20},{20,24},{24,28},{1,5},{5,9},{9,... | collective-permute-start | bytes 7864328 | tf_op jit(solution)/shard_map/ppermute | solution.py:21
  91.6 21.6 %all-to-all-start.2 = ((bf16[4,2,81920]{2,1,0:T(2,128)(2,1)}), bf16[4,2,81920]{2,1,0:T(2,128)(2,1)}, u32[]{:S(2)}, u32[]{:S(2)}) async-start(bf16[4,2,81920]{2,1,0:T(2,128)(2,1)} %reshape.320), calls=%async_computation.2 | async-start | bytes 2621440 | tf_op jit(solution)/shard_map/all_to_all | solution.py:102
  110.4 7.3 copy-start.17
  110.4 7.4 copy-start.14
  113.2 21.8 %all-to-all-start.4 = ((bf16[4,2,81920]{2,1,0:T(2,128)(2,1)}), bf16[4,2,81920]{2,1,0:T(2,128)(2,1)}, u32[]{:S(2)}, u32[]{:S(2)}) async-start(bf16[4,2,81920]{2,1,0:T(2,128)(2,1)} %reshape.322), calls=%async_computation.4 | async-start | bytes 2621440 | tf_op jit(solution)/shard_map/all_to_all | solution.py:105
  496.8 9.1 copy-start.13
  526.9 4.3 copy-start.16
  526.9 4.3 copy-start.19
  644.3 9.1 copy-start.13
  791.6 9.1 copy-start.13
  821.8 4.3 copy-start.16
  821.8 4.3 copy-start.19
  939.2 9.1 copy-start.13
  969.2 4.3 copy-start.16
  969.2 4.3 copy-start.19
  983.4 12.8 %copy-start.9 = (bf16[16,32,1280]{2,1,0:T(8,128)(2,1)S(1)}, bf16[16,32,1280]{2,1,0:T(8,128)(2,1)}, u32[]{:S(2)}) copy-start(bf16[16,32,1280]{2,1,0:T(8,128)(2,1)} %get-tuple-element.663) | copy-start | bytes 3932164
  988.7 61.4 %collective-permute-start.2 = (bf16[2,16,32,1280]{3,2,1,0:T(8,128)(2,1)}, bf16[2,16,32,1280]{3,2,1,0:T(8,128)(2,1)}, u32[]{:S(2)}, u32[]{:S(2)}) collective-permute-start(bf16[2,16,32,1280]{3,2,1,0:T(8,128)(2,1)} %get-tuple-element.360), channel_id=1, source_target_pairs={{4,0},{8,4},{12,8},{16,12},{20,16},{24,20},{28,24},{5,1},{9,5},{13... | collective-permute-start | bytes 7864328 | tf_op jit(solution)/shard_map/ppermute | solution.py:30
  990.0 116.5 %collective-permute-start.3 = (bf16[2,16,32,1280]{3,2,1,0:T(8,128)(2,1)}, bf16[2,16,32,1280]{3,2,1,0:T(8,128)(2,1)}, u32[]{:S(2)}, u32[]{:S(2)}) collective-permute-start(bf16[2,16,32,1280]{3,2,1,0:T(8,128)(2,1)} %get-tuple-element.361), channel_id=1, source_target_pairs={{0,4},{4,8},{8,12},{12,16},{16,20},{20,24},{24,28},{1,5},{5,9},{9,... | collective-permute-start | bytes 7864328 | tf_op jit(solution)/shard_map/ppermute | solution.py:30
  1015.9 99.0 %all-to-all-start.5 = ((bf16[16,32,1280]{2,1,0:T(8,128)(2,1)}), bf16[16,32,1280]{2,1,0:T(8,128)(2,1)}, u32[]{:S(2)}, u32[]{:S(2)}) async-start(bf16[16,32,1280]{2,1,0:T(8,128)(2,1)} %bitcast.20), calls=%async_computation.5 | async-start | bytes 2621440 | tf_op jit(solution)/shard_map/all_to_all | solution.py:194
  1135.3 20.8 %all-to-all-start.6 = ((bf16[16,32,1280]{2,1,0:T(8,128)(2,1)}), bf16[16,32,1280]{2,1,0:T(8,128)(2,1)S(1)}, u32[]{:S(2)}, u32[]{:S(2)}) async-start(bf16[16,32,1280]{2,1,0:T(8,128)(2,1)} %get-tuple-element.363), calls=%async_computation.6 | async-start | bytes 2621440 | tf_op jit(solution)/shard_map/all_to_all | solution.py:195
  (51 other events, 123.4 us)
where the time goes:
time: 1180 us; the launch traced here: 1160 us
  local copies, waits for them, and re-layouts  636 us (54%)
  other arithmetic  201 us (17%)
  waiting for transfers between devices  154 us (13%)
  matrix products  79.6 us (7%)
  blocking collectives  40.1 us (3%)
  starting transfers between devices  39.6 us (3%)
    concatenate x24, local copies, waits for them, and re-layouts, blocks(): jnp.concatenate((window[1], far_values), axis=1).reshape(four_dims)  98.9 us
    concatenate x24, local copies, waits for them, and re-layouts, blocks(): jnp.concatenate((window[0], far_keys), axis=1).reshape(four_dims)  93.1 us
    unnamed x23, local copies, waits for them, and re-layouts  89.2 us
    ppermute x2, waiting for transfers between devices, passed_along(): return lax.ppermute(block, axis, route)  86.3 us
    scatter-add x4, other arithmetic, backward_step(): far_sum = far_sum.at[:, rows_here.reshape(-1)].add(far_terms)  83.8 us
    another operation x4, other arithmetic, backward_step(): jnp.stack((key_grad, value_grad)).reshape(2, GROUP, key_count, columns)  48.5 us
    slice x4, local copies, waits for them, and re-layouts, backward_step(): key_terms[:, :, span_rows:]  45.3 us
    dynamic_update_slice x8, local copies, waits for them, and re-layouts, backward_step(): lax.dynamic_update_slice_in_dim(window_sum, key_terms[:, :, :span_rows],...  39.3 us
  transfers between devices with their start and end apart: 10, of which 8 were waited for; matrix products, arithmetic and copies ran while one was open for 8% of the time, Pallas kernels for 0%

commit v1 on v0

v1 whole, which is shorter than its diff:
```python
import functools
import math

import jax
import jax.numpy as jnp
from jax import lax
from jax.experimental import pallas as pl
from jax.experimental.pallas import tpu as pltpu
from jax.sharding import PartitionSpec as P

HD = 128
NEGATIVE = -1e30
MESH = pl.DeviceIdType.MESH
LANES = 128


def nt(a, b):
    return lax.dot_general(a, b, (((1,), (1,)), ((), ())), preferred_element_type=jnp.float32)


def nn(a, b):
    return jnp.dot(a, b, preferred_element_type=jnp.float32)


def kernel(
    dims,
    q_ref,
    k_ref,
    v_ref,
    g_ref,
    bias_ref,
    o_ref,
    dq_ref,
    dk_ref,
    dv_ref,
    buf,
    halo,
    obuf,
    gsend,
    grecv,
    acc,
    bias_buf,
    bias_full,
    prob_t,
    grad_t,
    in_send,
    in_recv,
    out_send,
    out_recv,
    halo_send,
    halo_recv,
    gh_send,
    gh_recv,
    bias_send,
    bias_recv,
):
    groups, merge, ranks, local_heads, frames, part, slab = dims
    members = merge * ranks
    length = frames * slab
    per_chunk = LANES // slab
    scale = HD ** (-0.5)
    log_scale = scale * math.log2(math.e)

    ctx = lax.axis_index("ctx")
    rank = lax.axis_index("head")
    group = lax.div(ctx, merge)
    inner = lax.rem(ctx, merge)
    me = inner * ranks + rank
    has_prev = group > 0
    has_next = group < groups - 1
    prev_id = (ctx - merge, rank)
    next_id = (ctx + merge, rank)

    def member(step):
        slot = lax.rem(me + step, members)
        return slot, (group * merge + lax.div(slot, ranks), lax.rem(slot, ranks))

    barrier = pltpu.get_barrier_semaphore()
    for step in range(1, members):
        pl.semaphore_signal(barrier, inc=1, device_id=member(step)[1], device_id_type=MESH)

    @pl.when(has_prev)
    def _():
        pl.semaphore_signal(barrier, inc=1, device_id=prev_id, device_id_type=MESH)

    @pl.when(has_next)
    def _():
        pl.semaphore_signal(barrier, inc=1, device_id=next_id, device_id_type=MESH)

    @pl.when(jnp.logical_not(has_prev))
    def _():
        halo[:, 0] = jnp.zeros(halo.shape[:1] + halo.shape[2:], halo.dtype)

    @pl.when(jnp.logical_not(has_next))
    def _():
        halo[:, 1] = jnp.zeros(halo.shape[:1] + halo.shape[2:], halo.dtype)

    pl.semaphore_wait(
        barrier, members - 1 + has_prev.astype(jnp.int32) + has_next.astype(jnp.int32)
    )

    def bias_copy(step):
        other = lax.rem(inner + step, merge)
        return pltpu.make_async_remote_copy(
            src_ref=bias_ref,
            dst_ref=bias_buf.at[inner],
            send_sem=bias_send.at[step],
            recv_sem=bias_recv.at[step],
            device_id=(group * merge + other, rank),
            device_id_type=MESH,
        )

    for step in range(1, merge):
        bias_copy(step).start()

    mine = pl.ds(me * part, part)

    @pl.loop(0, local_heads)
    def _(h):
        for step in list(range(1, members)) + [0]:
            slot, device = member(step)
            columns = pl.ds(pl.multiple_of((slot * local_heads + h) * HD, HD), HD)
            for a, source in ((1, k_ref), (2, v_ref), (0, q_ref), (3, g_ref)):
                src, dst = source.at[:, :, columns], buf.at[h, a, mine]
                if step:
                    pltpu.make_async_remote_copy(
                        src_ref=src,
                        dst_ref=dst,
                        send_sem=in_send,
                        recv_sem=in_recv.at[h],
                        device_id=device,
                        device_id_type=MESH,
                    ).start()
                else:
                    pltpu.make_async_copy(src, dst, in_recv.at[h]).start()

    bias_buf[inner] = bias_ref[...]
    for step in range(1, merge):
        bias_copy(step).wait()
    for s in range(merge):
        for frame in range(frames):
            bias_full[s, frame * slab : (frame + 1) * slab, :] = jnp.broadcast_to(
                bias_buf[s, frame : frame + 1, :], (slab, length)
            )

    last = (merge - 1) * frames

    def arrive(h):
        pltpu.make_async_copy(buf.at[h], buf.at[h], in_recv.at[h]).wait()

        @pl.when(has_next)
        def _():
            pltpu.make_async_remote_copy(
                src_ref=buf.at[h, pl.ds(1, 2), pl.ds(last, frames)],
                dst_ref=halo.at[h, 0],
                send_sem=halo_send.at[0],
                recv_sem=halo_recv.at[h, 0],
                device_id=next_id,
                device_id_type=MESH,
            ).start()

        @pl.when(has_prev)
        def _():
            pltpu.make_async_remote_copy(
                src_ref=buf.at[h, pl.ds(1, 2), pl.ds(0, frames)],
                dst_ref=halo.at[h, 1],
                send_sem=halo_send.at[1],
                recv_sem=halo_recv.at[h, 1],
                device_id=prev_id,
                device_id_type=MESH,
            ).start()

    def send_out(h, arrays):
        columns = pl.ds(pl.multiple_of((me * local_heads + h) * HD, HD), HD)
        for step in list(range(1, members)) + [0]:
            slot, device = member(step)
            for a, target in arrays:
                src, dst = obuf.at[h, a, pl.ds(slot * part, part)], target.at[:, :, columns]
                if step:
                    pltpu.make_async_remote_copy(
                        src_ref=src,
                        dst_ref=dst,
                        send_sem=out_send,
                        recv_sem=out_recv.at[a],
                        device_id=device,
                        device_id_type=MESH,
                    ).start()
                else:
                    pltpu.make_async_copy(src, dst, out_recv.at[a]).start()

    lane_frame = lax.div(lax.broadcasted_iota(jnp.int32, (slab, LANES), 1), slab)

    def compact(block):
        result = block[:slab]
        for i in range(1, per_chunk):
            result = jnp.where(lane_frame == i, block[i * slab : (i + 1) * slab], result)
        return result

    def expand(block):
        return jnp.concatenate(
            [jnp.where(lane_frame == i, block, 0.0) for i in range(per_chunk)], axis=0
        ).astype(jnp.bfloat16)

    def compute(h):
        @pl.when(has_prev)
        def _():
            pltpu.make_async_copy(halo.at[h, 0], halo.at[h, 0], halo_recv.at[h, 0]).wait()

        @pl.when(has_next)
        def _():
            pltpu.make_async_copy(halo.at[h, 1], halo.at[h, 1], halo_recv.at[h, 1]).wait()

        edge_prev = jnp.where(has_prev, 0.0, NEGATIVE)
        edge_next = jnp.where(has_next, 0.0, NEGATIVE)

        def rows_of(a, s):
            return buf[h, a, s * frames : (s + 1) * frames].reshape(length, HD)

        keys = [halo[h, 0, 0].reshape(length, HD)]
        values = [halo[h, 0, 1].reshape(length, HD)]
        for s in range(merge):
            keys.append(rows_of(1, s))
            values.append(rows_of(2, s))
        keys.append(halo[h, 1, 0].reshape(length, HD))
        values.append(halo[h, 1, 1].reshape(length, HD))
        keys_t = [x.T for x in keys]
        values_t = [x.T for x in values]

        acc[h] = jnp.zeros(acc.shape[1:], acc.dtype)

        def add_term(a, s, at, term):
            if s < 0 or s >= merge:
                side = 0 if s < 0 else 1
                first = at // slab
                gsend[h, side, a, first : first + per_chunk] = term.astype(jnp.bfloat16).reshape(
                    per_chunk, slab, HD
                )
            else:
                start = s * length + at
                acc[h, a, start : start + LANES] += term

        for s in range(merge):
            query, grad = rows_of(0, s), rows_of(3, s)
            own_k, own_v = keys[s + 1], values[s + 1]
            for at in range(0, length, LANES):
                rows = slice(at, at + LANES)
                q, g = query[rows], grad[rows]
                score = nt(own_k, q) * log_scale + bias_full[s, :, rows]
                score_p = compact(nt(keys[s][rows], q)) * log_scale
                score_n = compact(nt(keys[s + 2][rows], q)) * log_scale
                if s == 0:
                    score_p = score_p + edge_prev
                if s == merge - 1:
                    score_n = score_n + edge_next
                sides = jnp.maximum(score_p, score_n)
                top = jnp.maximum(
                    jnp.max(score, axis=0, keepdims=True), jnp.max(sides, axis=0, keepdims=True)
                )
                e, e_p, e_n = jnp.exp2(score - top), jnp.exp2(score_p - top), jnp.exp2(score_n - top)
                total = jnp.sum(e, axis=0, keepdims=True) + jnp.sum(
                    e_p + e_n, axis=0, keepdims=True
                )
                d = nt(own_v, g)
                d_p = compact(nt(values[s][rows], g))
                d_n = compact(nt(values[s + 2][rows], g))
                inv = 1.0 / total
                delta = inv * (
                    jnp.sum(e * d, axis=0, keepdims=True)
                    + jnp.sum(e_p * d_p + e_n * d_n, axis=0, keepdims=True)
                )
                inv_scale = inv * scale
                p = (e * inv).astype(jnp.bfloat16)
                ds = ((e * inv_scale) * (d - delta)).astype(jnp.bfloat16)
                p_p, p_n = expand(e_p * inv), expand(e_n * inv)
                ds_p = expand((e_p * inv_scale) * (d_p - delta))
                ds_n = expand((e_n * inv_scale) * (d_n - delta))
                prob_t[:, rows] = p
                grad_t[:, rows] = ds
                out_t = (
                    nn(values_t[s + 1], p)
                    + nn(values_t[s][:, rows], p_p)
                    + nn(values_t[s + 2][:, rows], p_n)
                )
                dq_t = (
                    nn(keys_t[s + 1], ds)
                    + nn(keys_t[s][:, rows], ds_p)
                    + nn(keys_t[s + 2][:, rows], ds_n)
                )
                first = s * frames + at // slab
                put = slice(first, first + per_chunk)
                obuf[h, 0, put] = out_t.T.astype(jnp.bfloat16).reshape(per_chunk, slab, HD)
                obuf[h, 1, put] = dq_t.T.astype(jnp.bfloat16).reshape(per_chunk, slab, HD)
                add_term(0, s - 1, at, nn(ds_p, q))
                add_term(1, s - 1, at, nn(p_p, g))
                add_term(0, s + 1, at, nn(ds_n, q))
                add_term(1, s + 1, at, nn(p_n, g))
            whole = slice(s * length, (s + 1) * length)
            acc[h, 0, whole] += nn(grad_t[...], query)
            acc[h, 1, whole] += nn(prob_t[...], grad)

        @pl.when(has_prev)
        def _():
            pltpu.make_async_remote_copy(
                src_ref=gsend.at[h, 0],
                dst_ref=grecv.at[h, 1],
                send_sem=gh_send.at[0],
                recv_sem=gh_recv.at[h, 1],
                device_id=prev_id,
                device_id_type=MESH,
            ).start()

        @pl.when(has_next)
        def _():
            pltpu.make_async_remote_copy(
                src_ref=gsend.at[h, 1],
                dst_ref=grecv.at[h, 0],
                send_sem=gh_send.at[1],
                recv_sem=gh_recv.at[h, 0],
                device_id=next_id,
                device_id_type=MESH,
            ).start()

        send_out(h, ((0, o_ref), (1, dq_ref)))

    def finish(h):
        for side, present, s in ((0, has_prev, 0), (1, has_next, merge - 1)):

            @pl.when(present)
            def _():
                pltpu.make_async_copy(
                    grecv.at[h, side], grecv.at[h, side], gh_recv.at[h, side]
                ).wait()
                term = grecv[h, side].astype(jnp.float32).reshape(2, length, HD)
                acc[h, :, s * length : (s + 1) * length] += term

        obuf[h, 2:4] = acc[h].astype(jnp.bfloat16).reshape(2, merge * frames, slab, HD)
        send_out(h, ((2, dk_ref), (3, dv_ref)))

    arrive(0)

    @pl.loop(0, local_heads)
    def _(h):
        @pl.when(h < local_heads - 1)
        def _():
            arrive(h + 1)

        compute(h)

        @pl.when(h > 0)
        def _():
            finish(h - 1)

    finish(local_heads - 1)

    sent = pl.ds(0, (members - 1) * part)
    pltpu.make_async_copy(buf.at[:, :, sent], buf.at[:, :, sent], in_send).wait()
    pltpu.make_async_copy(obuf.at[:, :, sent], obuf.at[:, :, sent], out_send).wait()
    for a, target in enumerate((o_ref, dq_ref, dk_ref, dv_ref)):
        pltpu.make_async_copy(target, target, out_recv.at[a]).wait()

    @pl.when(has_next)
    def _():
        pltpu.make_async_copy(halo.at[:, 0], halo.at[:, 0], halo_send.at[0]).wait()
        pltpu.make_async_copy(gsend.at[:, 1], gsend.at[:, 1], gh_send.at[1]).wait()

    @pl.when(has_prev)
    def _():
        pltpu.make_async_copy(halo.at[:, 1], halo.at[:, 1], halo_send.at[1]).wait()
        pltpu.make_async_copy(gsend.at[:, 0], gsend.at[:, 0], gh_send.at[0]).wait()


def frame_bias(slot_frames, frame_order, slab):
    frame_ids = jnp.arange(frame_order.shape[0], dtype=jnp.int32)
    one_hot = (frame_order[:, None] == frame_ids[None, :]).astype(jnp.int32)
    picked = jnp.sum(one_hot[:, :, None] * slot_frames[None, :, :], axis=1)
    hit = jnp.any(picked[None, :, :] == frame_order[:, None, None], axis=2)
    hit = hit | (frame_ids[:, None] == frame_ids[None, :])
    return jnp.repeat(jnp.where(hit, 0.0, NEGATIVE).astype(jnp.float32), slab, axis=1)


def on_device(queries, keys, values, out_grad, band_frames, frame_order):
    part, slab, columns = queries.shape
    frames = frame_order.shape[0]
    ranks = lax.axis_size("head")
    slabs = lax.axis_size("ctx")
    heads = columns // HD
    merge = math.gcd(heads // ranks, slabs)
    local_heads = heads // (ranks * merge)
    length = frames * slab
    dims = (slabs // merge, merge, ranks, local_heads, frames, part, slab)
    bias = frame_bias(band_frames[:, 0, :], frame_order, slab)
    spread = (local_heads, 4, merge * frames, slab, HD)
    edge = (local_heads, 2, 2, frames, slab, HD)
    any_spec = pl.BlockSpec(memory_space=pl.ANY)
    width = length + 2 * LANES
    outs = pl.pallas_call(
        functools.partial(kernel, dims),
        out_shape=[jax.ShapeDtypeStruct(queries.shape, queries.dtype)] * 4,
        in_specs=[any_spec] * 4 + [pl.BlockSpec(memory_space=pltpu.VMEM)],
        out_specs=[any_spec] * 4,
        scratch_shapes=[
            pltpu.VMEM(spread, jnp.bfloat16),
            pltpu.VMEM(edge, jnp.bfloat16),
            pltpu.VMEM(spread, jnp.bfloat16),
            pltpu.VMEM(edge, jnp.bfloat16),
            pltpu.VMEM(edge, jnp.bfloat16),
            pltpu.VMEM((local_heads, 2, merge * length, HD), jnp.float32),
            pltpu.VMEM((merge, frames, length), jnp.float32),
            pltpu.VMEM((merge, length, length), jnp.float32),
            pltpu.VMEM((length, length), jnp.bfloat16),
            pltpu.VMEM((length, length), jnp.bfloat16),
            pltpu.SemaphoreType.DMA,
            pltpu.SemaphoreType.DMA((local_heads,)),
            pltpu.SemaphoreType.DMA,
            pltpu.SemaphoreType.DMA((4,)),
            pltpu.SemaphoreType.DMA((2,)),
            pltpu.SemaphoreType.DMA((local_heads, 2)),
            pltpu.SemaphoreType.DMA((2,)),
            pltpu.SemaphoreType.DMA((local_heads, 2)),
            pltpu.SemaphoreType.DMA((merge,)),
            pltpu.SemaphoreType.DMA((merge,)),
        ],
        compiler_params=pltpu.CompilerParams(
            collective_id=0, has_side_effects=True, vmem_limit_bytes=50 * 1024 * 1024
        ),
        cost_estimate=pl.CostEstimate(
            flops=12 * local_heads * merge * length * width * HD,
            bytes_accessed=16 * part * slab * columns,
            transcendentals=local_heads * merge * length * width,
        ),
    )(queries, keys, values, out_grad, bias)
    return tuple(outs)


def solution(mesh):
    wide = P("head", "ctx", None)
    return jax.shard_map(
        on_device,
        mesh=mesh,
        in_specs=(wide, wide, wide, wide, P(None, "ctx", None), P()),
        out_specs=(wide,) * 4,
        check_vma=False,
    )
```

time: 1180 us -> 127 us (0.11); the launches traced: 1160 us -> 127 us
  local copies, waits for them, and re-layouts: 636 us -> 5.22 us
  other arithmetic: 201 us -> 2.53 us
  waiting for transfers between devices: 154 us -> 0 us
  Pallas kernels: 0 us -> 119 us
  matrix products: 79.6 us -> 0 us
  blocking collectives: 40.1 us -> 0 us
  starting transfers between devices: 39.6 us -> 0 us
    concatenate x56 -> x0, local copies, waits for them, and re-layouts: 192 us -> none  [the longest x24 98.9 us: blocks(): jnp.concatenate((window[1], far_values), axis=1).reshape(four_dims)]
    ppermute x4 -> x0, waiting for transfers between devices: 125 us -> none  [the longest x2 86.3 us: passed_along(): return lax.ppermute(block, axis, route)]
    pallas_call x0 -> x1, Pallas kernels: none -> 119 us  [on_device(): pl.pallas_call(functools.partial(kernel, dims), out_shape=[jax.ShapeDtype...]
    unnamed x23 -> x6, local copies, waits for them, and re-layouts: 89.2 us -> 4.96 us
    scatter-add x4 -> x0, other arithmetic: 83.8 us -> none  [backward_step(): far_sum = far_sum.at[:, rows_here.reshape(-1)].add(far_terms)]
    dot_general x28 -> x0, matrix products: 79.6 us -> none  [the longest x4 22.4 us: backward_group(): jnp.einsum('ghqk,gqhd->gkhd', weights, grad_block, preferred_element_type...]
    slice x13 -> x0, local copies, waits for them, and re-layouts: 77.7 us -> none  [the longest x4 45.3 us: backward_step(): key_terms[:, :, span_rows:]]
    transpose x12 -> x0, local copies, waits for them, and re-layouts: 71.2 us -> none  [the longest x4 35.6 us: backward_group(): jnp.einsum('ghqk,gqhd->gkhd', score_grads, query_block, preferred_element...]
  transfers between devices with their start and end apart: 10 -> 0, of which waited for: 8 -> 0; matrix products, arithmetic and copies ran while one was open for 8% -> 0% of each run, Pallas kernels for 0% -> 0%
where the time goes in v1:
time: 127 us
  Pallas kernels  119 us (94%)
  local copies, waits for them, and re-layouts  5.22 us (4%)
  other arithmetic  2.53 us (2%)
    pallas_call x1, Pallas kernels, on_device(): pl.pallas_call(functools.partial(kernel, dims), out_shape=[jax.ShapeDtype...  119 us
    unnamed x6, local copies, waits for them, and re-layouts  4.96 us

profile of v1, /device:TPU:0, one launch (start us, length us, event | category | flops | bytes accessed | tf_op | source)
XLA Modules:
  0.0 127.0 jit_solution(6855935019438812681)
XLA Ops:
  0.6 0.7 fusion
  1.4 1.0 multiply_reduce_fusion
  2.4 0.1 copy.11
  2.5 0.8 compare_reduce_fusion
  3.2 0.1 broadcast_in_dim.20
  3.3 0.1 reshape.36.bias_ref
  3.4 118.5 %shard_map.93 = (bf16[4,32,5120]{2,1,0:T(8,128)(2,1)S(1)}, bf16[4,32,5120]{2,1,0:T(8,128)(2,1)S(1)}, bf16[4,32,5120]{2,1,0:T(8,128)(2,1)S(1)}, bf16[4,32,5120]{2,1,0:T(8,128)(2,1)}) custom-call(bf16[4,32,5120]{2,1,0:T(8,128)(2,1)} %q_ref.1, bf16[4,32,5120]{2,1,0:T(8,128)(2,1)} %k_ref.1, bf16[4,32,5120]{2,1,0:T(8,128)(2,1)} %v_ref.1, ...), custom_call_target="tpu_custom_call" | custom-call | flops 6039797760 | bytes 10485760 | tf_op jit(solution)/shard_map/pallas_call | solution.py:396
  122.0 1.1 copy.16
  123.1 1.1 copy.17
  124.1 0.0 copy-start
  124.1 1.1 copy.18
  125.2 0.7 copy-done
  125.9 1.1 copy.19
  (1 shorter events, 0.0 us)
Async XLA Ops:
  124.1 1.8 %copy-start = (bf16[4,32,5120]{2,1,0:T(8,128)(2,1)S(1)}, bf16[4,32,5120]{2,1,0:T(8,128)(2,1)}, u32[]{:S(2)}) copy-start(bf16[4,32,5120]{2,1,0:T(8,128)(2,1)} %get-tuple-element.11) | copy-start | bytes 3932164

commit v2 on v1

--- a/solution.py
+++ b/solution.py
@@ -28,7 +28,8 @@
     k_ref,
     v_ref,
     g_ref,
-    bias_ref,
+    band_hbm,
+    order_hbm,
     o_ref,
     dq_ref,
     dk_ref,
@@ -53,6 +54,10 @@
     gh_recv,
     bias_send,
     bias_recv,
+    band_ref,
+    order_ref,
+    band_sem,
+    order_sem,
 ):
     groups, merge, ranks, local_heads, frames, part, slab = dims
     members = merge * ranks
@@ -102,7 +107,7 @@
     def bias_copy(step):
         other = lax.rem(inner + step, merge)
         return pltpu.make_async_remote_copy(
-            src_ref=bias_ref,
+            src_ref=bias_buf.at[inner],
             dst_ref=bias_buf.at[inner],
             send_sem=bias_send.at[step],
             recv_sem=bias_recv.at[step],
@@ -110,13 +115,9 @@
             device_id_type=MESH,
         )
 
-    for step in range(1, merge):
-        bias_copy(step).start()
-
     mine = pl.ds(me * part, part)
 
-    @pl.loop(0, local_heads)
-    def _(h):
+    def send_in(h):
         for step in list(range(1, members)) + [0]:
             slot, device = member(step)
             columns = pl.ds(pl.multiple_of((slot * local_heads + h) * HD, HD), HD)
@@ -134,7 +135,33 @@
                 else:
                     pltpu.make_async_copy(src, dst, in_recv.at[h]).start()
 
-    bias_buf[inner] = bias_ref[...]
+    send_in(0)
+
+    band_copy = pltpu.make_async_copy(band_hbm, band_ref, band_sem)
+    order_copy = pltpu.make_async_copy(order_hbm, order_ref, order_sem)
+    band_copy.start()
+    order_copy.start()
+    band_copy.wait()
+    order_copy.wait()
+    row_at = lax.broadcasted_iota(jnp.int32, (frames, length), 0)
+    lane_at = lax.div(lax.broadcasted_iota(jnp.int32, (frames, length), 1), slab)
+    order_rows = jnp.zeros((frames, length), jnp.int32)
+    for p in range(frames):
+        order_rows = jnp.where(row_at == p, order_ref[p], order_rows)
+    hit = row_at == lane_at
+    for slot in range(band_ref.shape[1]):
+        wanted = jnp.full((frames, length), -1, jnp.int32)
+        for p in range(frames):
+            wanted = jnp.where(lane_at == p, band_ref[0, slot, order_ref[p]], wanted)
+        hit = jnp.logical_or(hit, wanted == order_rows)
+    bias_buf[inner] = jnp.where(hit, 0.0, NEGATIVE)
+    for step in range(1, merge):
+        bias_copy(step).start()
+
+    @pl.loop(1, local_heads)
+    def _(h):
+        send_in(h)
+
     for step in range(1, merge):
         bias_copy(step).wait()
     for s in range(merge):
@@ -369,13 +396,22 @@
         pltpu.make_async_copy(gsend.at[:, 0], gsend.at[:, 0], gh_send.at[0]).wait()
 
 
-def frame_bias(slot_frames, frame_order, slab):
-    frame_ids = jnp.arange(frame_order.shape[0], dtype=jnp.int32)
-    one_hot = (frame_order[:, None] == frame_ids[None, :]).astype(jnp.int32)
-    picked = jnp.sum(one_hot[:, :, None] * slot_frames[None, :, :], axis=1)
-    hit = jnp.any(picked[None, :, :] == frame_order[:, None, None], axis=2)
-    hit = hit | (frame_ids[:, None] == frame_ids[None, :])
-    return jnp.repeat(jnp.where(hit, 0.0, NEGATIVE).astype(jnp.float32), slab, axis=1)
+def place(*refs):
+    count = (len(refs) - 3) // 2
+    held, read_sem, write_sem = refs[-3:]
+    reads, writes = [], []
+    for i in range(count):
+        src, dst = refs[i], refs[count + i]
+        for j in range(src.shape[0]):
+            reads.append(pltpu.make_async_copy(src.at[j], held.at[i, j], read_sem.at[i, j]))
+            writes.append(pltpu.make_async_copy(held.at[i, j], dst.at[j], write_sem.at[i, j]))
+    for copy in reads:
+        copy.start()
+    for read, write in zip(reads, writes):
+        read.wait()
+        write.start()
+    for copy in writes:
+        copy.wait()
 
 
 def on_device(queries, keys, values, out_grad, band_frames, frame_order):
@@ -388,7 +424,6 @@
     local_heads = heads // (ranks * merge)
     length = frames * slab
     dims = (slabs // merge, merge, ranks, local_heads, frames, part, slab)
-    bias = frame_bias(band_frames[:, 0, :], frame_order, slab)
     spread = (local_heads, 4, merge * frames, slab, HD)
     edge = (local_heads, 2, 2, frames, slab, HD)
     any_spec = pl.BlockSpec(memory_space=pl.ANY)
@@ -396,7 +431,7 @@
     outs = pl.pallas_call(
         functools.partial(kernel, dims),
         out_shape=[jax.ShapeDtypeStruct(queries.shape, queries.dtype)] * 4,
-        in_specs=[any_spec] * 4 + [pl.BlockSpec(memory_space=pltpu.VMEM)],
+        in_specs=[pl.BlockSpec(memory_space=pltpu.HBM)] * 6,
         out_specs=[any_spec] * 4,
         scratch_shapes=[
             pltpu.VMEM(spread, jnp.bfloat16),
@@ -419,17 +454,33 @@
             pltpu.SemaphoreType.DMA((local_heads, 2)),
             pltpu.SemaphoreType.DMA((merge,)),
             pltpu.SemaphoreType.DMA((merge,)),
+            pltpu.SMEM((1, band_frames.shape[2], frames), jnp.int32),
+            pltpu.SMEM((frames,), jnp.int32),
+            pltpu.SemaphoreType.DMA,
+            pltpu.SemaphoreType.DMA,
         ],
         compiler_params=pltpu.CompilerParams(
-            collective_id=0, has_side_effects=True, vmem_limit_bytes=50 * 1024 * 1024
+            collective_id=0, has_side_effects=True, vmem_limit_bytes=58 * 1024 * 1024
         ),
         cost_estimate=pl.CostEstimate(
             flops=12 * local_heads * merge * length * width * HD,
             bytes_accessed=16 * part * slab * columns,
             transcendentals=local_heads * merge * length * width,
         ),
-    )(queries, keys, values, out_grad, bias)
-    return tuple(outs)
+    )(queries, keys, values, out_grad, jnp.transpose(band_frames, (1, 2, 0)), frame_order)
+    placed = pl.pallas_call(
+        place,
+        out_shape=[jax.ShapeDtypeStruct(x.shape, x.dtype) for x in outs],
+        in_specs=[pl.BlockSpec(memory_space=pltpu.HBM)] * 4,
+        out_specs=[pl.BlockSpec(memory_space=pltpu.HBM)] * 4,
+        scratch_shapes=[
+            pltpu.VMEM((4, part, slab, columns), queries.dtype),
+            pltpu.SemaphoreType.DMA((4, part)),
+            pltpu.SemaphoreType.DMA((4, part)),
+        ],
+        compiler_params=pltpu.CompilerParams(vmem_limit_bytes=58 * 1024 * 1024),
+    )(*outs)
+    return tuple(placed)
 
 
 def solution(mesh):

time: 127 us -> 125 us (0.984)
  local copies, waits for them, and re-layouts: 5.22 us -> 0 us
  Pallas kernels: 119 us -> 124 us
  other arithmetic: 2.53 us -> 0 us
    unnamed x6 -> x0, local copies, waits for them, and re-layouts: 4.96 us -> none
    pallas_call x0 -> x1, Pallas kernels: none -> 4.93 us  [on_device(): pl.pallas_call(place, out_shape=[jax.ShapeDtypeStruct(x.shape, x.dtype) f...]
where the time goes in v2:
time: 125 us; the launch traced here: 124 us
  Pallas kernels  124 us (99%)
    pallas_call x1, Pallas kernels, on_device(): pl.pallas_call(functools.partial(kernel, dims), out_shape=[jax.ShapeDtype...  119 us
    pallas_call x1, Pallas kernels, on_device(): pl.pallas_call(place, out_shape=[jax.ShapeDtypeStruct(x.shape, x.dtype) f...  4.93 us

profile of v2, /device:TPU:0, one launch (start us, length us, event | category | flops | bytes accessed | tf_op | source)
XLA Modules:
  0.0 124.3 jit_solution(3884857371256412915)
XLA Ops:
  0.6 118.8 %shard_map.93 = (bf16[4,32,5120]{2,1,0:T(8,128)(2,1)}, bf16[4,32,5120]{2,1,0:T(8,128)(2,1)}, bf16[4,32,5120]{2,1,0:T(8,128)(2,1)}, bf16[4,32,5120]{2,1,0:T(8,128)(2,1)}) custom-call(bf16[4,32,5120]{2,1,0:T(8,128)(2,1)} %q_ref.1, bf16[4,32,5120]{2,1,0:T(8,128)(2,1)} %k_ref.1, bf16[4,32,5120]{2,1,0:T(8,128)(2,1)} %v_ref.1, bf16[4,32,5120]{2,1,0:T(8,128)(2,1)} %g_ref.1, ...), custom_call_target="tpu_custom_call" | custom-call | flops 6039797760 | bytes 10485760 | tf_op jit(solution)/shard_map/pallas_call | solution.py:431
  119.4 4.9 %shard_map.94 = (bf16[4,32,5120]{2,1,0:T(8,128)(2,1)}, bf16[4,32,5120]{2,1,0:T(8,128)(2,1)}, bf16[4,32,5120]{2,1,0:T(8,128)(2,1)}, bf16[4,32,5120]{2,1,0:T(8,128)(2,1)}) custom-call(bf16[4,32,5120]{2,1,0:T(8,128)(2,1)} %get-tuple-element.8.refs_0_, bf16[4,32,5120]{2,1,0:T(8,128)(2,1)} %get-tuple-element.9.refs_1_, ...), custom_call_target="tpu_custom_call" | custom-call | tf_op jit(solution)/shard_map/pallas_call | solution.py:471

commit v3 on v2

--- a/solution.py
+++ b/solution.py
@@ -397,20 +397,16 @@
 
 
 def place(*refs):
-    count = (len(refs) - 3) // 2
-    held, read_sem, write_sem = refs[-3:]
-    reads, writes = [], []
+    count = (len(refs) - 1) // 2
+    sems = refs[-1]
+    copies = []
     for i in range(count):
         src, dst = refs[i], refs[count + i]
         for j in range(src.shape[0]):
-            reads.append(pltpu.make_async_copy(src.at[j], held.at[i, j], read_sem.at[i, j]))
-            writes.append(pltpu.make_async_copy(held.at[i, j], dst.at[j], write_sem.at[i, j]))
-    for copy in reads:
+            copies.append(pltpu.make_async_copy(src.at[j], dst.at[j], sems.at[i, j]))
+    for copy in copies:
         copy.start()
-    for read, write in zip(reads, writes):
-        read.wait()
-        write.start()
-    for copy in writes:
+    for copy in copies:
         copy.wait()
 
 
@@ -460,7 +456,7 @@
             pltpu.SemaphoreType.DMA,
         ],
         compiler_params=pltpu.CompilerParams(
-            collective_id=0, has_side_effects=True, vmem_limit_bytes=58 * 1024 * 1024
+            collective_id=0, has_side_effects=True, vmem_limit_bytes=48 * 1024 * 1024
         ),
         cost_estimate=pl.CostEstimate(
             flops=12 * local_heads * merge * length * width * HD,
@@ -471,14 +467,10 @@
     placed = pl.pallas_call(
         place,
         out_shape=[jax.ShapeDtypeStruct(x.shape, x.dtype) for x in outs],
-        in_specs=[pl.BlockSpec(memory_space=pltpu.HBM)] * 4,
+        in_specs=[pl.BlockSpec(memory_space=pltpu.VMEM)] * 4,
         out_specs=[pl.BlockSpec(memory_space=pltpu.HBM)] * 4,
-        scratch_shapes=[
-            pltpu.VMEM((4, part, slab, columns), queries.dtype),
-            pltpu.SemaphoreType.DMA((4, part)),
-            pltpu.SemaphoreType.DMA((4, part)),
-        ],
-        compiler_params=pltpu.CompilerParams(vmem_limit_bytes=58 * 1024 * 1024),
+        scratch_shapes=[pltpu.SemaphoreType.DMA((4, part))],
+        compiler_params=pltpu.CompilerParams(vmem_limit_bytes=8 * 1024 * 1024),
     )(*outs)
     return tuple(placed)
 

time: 125 us -> 123 us (0.984)
  Pallas kernels: 124 us -> 121 us
  local copies, waits for them, and re-layouts: 0 us -> 1.33 us
    pallas_call x1, Pallas kernels: 4.93 us -> 2.46 us  [on_device(): pl.pallas_call(place, out_shape=[jax.ShapeDtypeStruct(x.shape, x.dtype) f...]
    unnamed x0 -> x4, local copies, waits for them, and re-layouts: none -> 1.33 us
where the time goes in v3:
time: 123 us
  Pallas kernels  121 us (98%)
  local copies, waits for them, and re-layouts  1.33 us (1%)
    pallas_call x1, Pallas kernels, on_device(): pl.pallas_call(functools.partial(kernel, dims), out_shape=[jax.ShapeDtype...  119 us
    pallas_call x1, Pallas kernels, on_device(): pl.pallas_call(place, out_shape=[jax.ShapeDtypeStruct(x.shape, x.dtype) f...  2.46 us

profile of v3, /device:TPU:0, one launch (start us, length us, event | category | flops | bytes accessed | tf_op | source)
XLA Modules:
  0.0 123.1 jit_solution(14620930765698291580)
XLA Ops:
  0.6 0.0 copy-start
  0.6 0.7 copy-done
  1.3 0.0 copy-start.1
  1.3 0.7 copy-done.1
  2.0 118.7 %shard_map.93 = (bf16[4,32,5120]{2,1,0:T(8,128)(2,1)S(1)}, bf16[4,32,5120]{2,1,0:T(8,128)(2,1)S(1)}, bf16[4,32,5120]{2,1,0:T(8,128)(2,1)S(1)}, bf16[4,32,5120]{2,1,0:T(8,128)(2,1)S(1)}) custom-call(bf16[4,32,5120]{2,1,0:T(8,128)(2,1)} %q_ref.1, bf16[4,32,5120]{2,1,0:T(8,128)(2,1)} %k_ref.1, bf16[4,32,5120]{2,1,0:T(8,128)(2,1)} %v_ref.1, ...), custom_call_target="tpu_custom_call" | custom-call | flops 6039797760 | bytes 10485760 | tf_op jit(solution)/shard_map/pallas_call | solution.py:427
  120.7 2.5 %shard_map.94 = (bf16[4,32,5120]{2,1,0:T(8,128)(2,1)}, bf16[4,32,5120]{2,1,0:T(8,128)(2,1)}, bf16[4,32,5120]{2,1,0:T(8,128)(2,1)}, bf16[4,32,5120]{2,1,0:T(8,128)(2,1)}) custom-call(bf16[4,32,5120]{2,1,0:T(8,128)(2,1)S(1)} %get-tuple-element.8.refs_0_, bf16[4,32,5120]{2,1,0:T(8,128)(2,1)S(1)} %get-tuple-element.9.refs_1_, ...), custom_call_target="tpu_custom_call" | custom-call | tf_op jit(solution)/shard_map/pallas_call | solution.py:467
Async XLA Ops:
  0.6 0.7 copy-start
  1.3 0.7 copy-start.1
